TPU v7x, 32 devices: a whole 2x2x4 slice. The times are simulated.
32 devices in a mesh: row: 4 (over y, x), col: 8 (over z, core).
Axes of the slice: x: 2, y: 2, z: 4, core: 2. Of those that a mesh axis runs over, the one named last changes fastest.
Arguments:
- source_amps: float32 [1024, 6144], P(('row', 'col')), may hold values from -6 to 6
- row_owner: int32 [4, 256], replicated, may hold values from 0 to 255, each once within a row
- integrals: float32 [6144, 2048], P('row', 'col'), may hold values from -0.078125 to 0.078125
- occ_energy: float32 [1024], P('row'), may hold values from -2 to -0.5
- vir_energy: float32 [2048], P('col'), may hold values from 0.5 to 3
Outputs:
- increment: float32 [1024, 2048], P('row', 'col')
Inputs may be any that keep to these rules, and one draw needn't show every extreme that they name: Each row of row_owner holds every number below 256 once.
All inputs are finite; a program needn't handle non-finite values.
Results may differ from a plain program's by a relative error of at most 0.00007.
Values sent between devices are 32-bit elements; how exact they have to be, the bound alone decides.
A program may use at most 64 MiB of HBM per device.

v0:
```python
import jax
import jax.numpy as jnp
from jax import lax
from jax.sharding import PartitionSpec as P


def place_rows(block_rows, owners):
    return jnp.zeros_like(block_rows).at[owners].set(block_rows)


def per_device(source_amps, row_owner, integrals, occ_energy, vir_energy):
    owners = lax.dynamic_index_in_dim(row_owner, lax.axis_index("row"), 0, keepdims=False)
    arrived = lax.all_to_all(source_amps, "col", split_axis=1, concat_axis=0, tiled=True)
    ordered = place_rows(arrived, owners)
    amplitudes = lax.all_gather(ordered, "col", axis=1, tiled=True)
    ladder = jnp.dot(
        amplitudes,
        lax.all_gather(integrals, "row", axis=0, tiled=True),
        precision=lax.Precision.HIGHEST,
        preferred_element_type=jnp.float32,
    )
    return ladder / (vir_energy[None, :] - occ_energy[:, None])


def solution(mesh):
    return jax.shard_map(
        per_device,
        mesh=mesh,
        in_specs=(P(("row", "col"), None), P(), P("row", "col"), P("row"), P("col")),
        out_specs=P("row", "col"),
        check_vma=False,
    )
```

profile of v0, /device:TPU:0, one launch (start us, length us, event | category | flops | bytes accessed | tf_op | source)
XLA Modules:
  0.0 165.9 jit_solution(4610472822640494194)
XLA Ops:
  6.5 0.0 copy-start
  6.5 0.0 copy-start.1
  6.5 0.0 all-gather.5.cloned.1.call-start
  6.5 0.7 all-gather.5.cloned.1.call-update
  7.3 2.1 %copy.10 = f32[4,8,8,768]{3,2,0,1:T(8,128)} copy(f32[4,8,8,768]{3,2,1,0:T(8,128)} %bitcast.12) | data formatting | bytes 1572864 | tf_op jit(solution)/shard_map/all_to_all | solution.py:13
  9.4 6.3 %all-to-all-start = ((f32[32,8,768]{2,0,1:T(8,128)}), f32[32,8,768]{2,0,1:T(8,128)S(1)}, u32[]{:S(2)}, u32[]{:S(2)}) async-start(f32[32,8,768]{2,0,1:T(8,128)} %bitcast.11), calls=%async_computation | async-start | bytes 1572864 | tf_op jit(solution)/shard_map/all_to_all | solution.py:13
  15.7 0.0 all-gather.3.cloned.1.call-start
  15.7 0.7 compare_select_fusion
  16.4 20.2 %all-to-all-done = f32[32,8,768]{2,0,1:T(8,128)S(1)} async-done(((f32[32,8,768]{2,0,1:T(8,128)}), f32[32,8,768]{2,0,1:T(8,128)S(1)}, u32[]{:S(2)}, u32[]{:S(2)}) %all-to-all-start) | async-done | bytes 786464 | tf_op jit(solution)/shard_map/all_to_all | solution.py:13
  36.7 2.4 %scatter_custom_fusion = f32[256,768]{1,0:T(8,128)} fusion(s32[256]{0:T(256)S(1)} %bitcast.14, f32[256,768]{1,0:T(8,128)S(1)} %bitcast.13, f32[]{:T(128)} %constant.5.clone.1), kind=kCustom, calls=%fused_computation.3 | custom fusion | bytes 786436 | tf_op jit(solution)/shard_map/scatter | solution.py:8
  39.0 0.0 all-gather.3.cloned.1.call-update
  39.1 43.0 %all-gather.5.cloned.1.call-done = f32[6144,256]{1,0:T(8,128)} async-done(((f32[1536,256]{1,0:T(8,128)}), f32[6144,256]{1,0:T(8,128)}) %all-gather.5.cloned.1.call-update) | async-done | bytes 6291472 | tf_op jit(solution)/shard_map/all_gather | solution.py:18
  82.1 66.4 %all-gather.3.cloned.1.call-done = f32[256,6144]{1,0:T(8,128)} async-done(((f32[256,768]{1,0:T(8,128)}), f32[256,6144]{1,0:T(8,128)}) %all-gather.3.cloned.1.call-update) | async-done | bytes 6291472 | tf_op jit(solution)/shard_map/all_gather | solution.py:15
  148.5 0.0 copy-done
  148.5 0.0 copy-done.1
  148.5 10.6 %convolution_divide_fusion = f32[256,256]{1,0:T(8,128)} fusion(f32[256,6144]{1,0:T(8,128)} %all-gather.3.cloned.1.call-done, f32[6144,256]{1,0:T(8,128)} %all-gather.5.cloned.1.call-done, f32[256]{0:T(256)S(1)} %copy-done, f32[256]{0:T(256)S(1)} %copy-done.1), kind=kOutput, calls=%fused_computation.1 | convolution fusion | flops 4831969280 | bytes 12847104 | tf_op jit(solution)/shard_map/dot_general | solution.py:16
Async XLA Ops:
  6.5 141.9 %copy-start = (f32[256]{0:T(256)S(1)}, f32[256]{0:T(256)}, u32[]{:S(2)}) copy-start(f32[256]{0:T(256)} %param.8) | copy-start | bytes 3076
  6.5 141.9 %copy-start.1 = (f32[256]{0:T(256)S(1)}, f32[256]{0:T(256)}, u32[]{:S(2)}) copy-start(f32[256]{0:T(256)} %param.9) | copy-start | bytes 3076
  6.5 75.6 %all-gather.5.cloned.1.call-start = ((), (), s32[]{:S(2)}) async-start(), calls=%async_computation.2 | async-start | bytes 7864320 | tf_op jit(solution)/shard_map/all_gather | solution.py:18
  9.4 27.3 %all-to-all-start = ((f32[32,8,768]{2,0,1:T(8,128)}), f32[32,8,768]{2,0,1:T(8,128)S(1)}, u32[]{:S(2)}, u32[]{:S(2)}) async-start(f32[32,8,768]{2,0,1:T(8,128)} %bitcast.11), calls=%async_computation | async-start | bytes 1572864 | tf_op jit(solution)/shard_map/all_to_all | solution.py:13
  15.7 132.8 %all-gather.3.cloned.1.call-start = ((), (), s32[]{:S(2)}) async-start(), calls=%async_computation.1 | async-start | bytes 7077888 | tf_op jit(solution)/shard_map/all_gather | solution.py:15
Sparse Core Ops, SparseCore 0:
  9.2 72.8 all-gather.4
  83.7 64.7 all-gather.2
where the time goes:
time: 166 us
  waiting for transfers between devices  130 us (78%)
  between operations  13.4 us (8%)
  matrix products  10.6 us (6%)
  starting transfers between devices  6.36 us (4%)
  local copies, waits for them, and re-layouts  4.47 us (3%)
    all_gather x1, waiting for transfers between devices, per_device(): amplitudes = lax.all_gather(ordered, 'col', axis=1, tiled=True)  66.4 us
    all_gather x1, waiting for transfers between devices, per_device(): lax.all_gather(integrals, 'row', axis=0, tiled=True)  43 us
    all_to_all x1, waiting for transfers between devices, per_device(): lax.all_to_all(source_amps, 'col', split_axis=1, concat_axis=0, tiled=True)  20.2 us
    dot_general x1, matrix products, per_device(): jnp.dot(amplitudes, lax.all_gather(integrals, 'row', axis=0, tiled=True),...  10.6 us
    all_to_all x1, starting transfers between devices, per_device(): lax.all_to_all(source_amps, 'col', split_axis=1, concat_axis=0, tiled=True)  6.33 us
  transfers between devices with their start and end apart: 3, of which 3 were waited for; matrix products, arithmetic and copies ran while one was open for 3% of the time, Pallas kernels for 0%

commit v1 on v0

v1 whole, which is shorter than its diff:
```python
import functools

import jax
import jax.numpy as jnp
from jax import lax
from jax.experimental import pallas as pl
from jax.experimental.pallas import tpu as pltpu
from jax.sharding import PartitionSpec as P

MESH = pl.DeviceIdType.MESH
TAIL_PART = (0, 12)


def split2(x):
    hi = x.astype(jnp.bfloat16)
    return hi, (x - hi.astype(jnp.float32)).astype(jnp.bfloat16)


def dot(a, b):
    return jnp.dot(a, b, preferred_element_type=jnp.float32)


def flip(r, j, n):
    out, bit = 0, 1
    while bit < n:
        rb, jb = (r // bit) % 2, (j // bit) % 2
        out = out + bit * (rb + jb - 2 * rb * jb)
        bit *= 2
    return out


def kernel(
    R, Z, F,
    amps, owner, integrals, occ, vir, out,
    a_all, b_raw, b_hi, b_lo, part, slots, ladder, off_raw, off_hi, off_lo, off_part, off_slots, off_sum,
    own_recv, mate_recv, slot_recv, right_send, left_send, mate_send, slot_send, swap_send, load_sem,
    off_recv, off_send, sum_send, b_send, b_recv,
):
    r = lax.axis_index("row")
    c = lax.axis_index("col")
    z, co = c // 2, c % 2
    D = amps.shape[0]
    Kr = integrals.shape[0]
    H = Kr - F
    E = Z * R
    rows = 2 * D
    lower = (z < Z // 2).astype(jnp.int32)
    way = 2 * lower - 1
    n_out = jnp.minimum(z, Z - 1 - z)
    at_end = n_out == 0
    beside_end = n_out == 1
    end_z = (1 - lower) * (Z - 1)

    def event(e):
        f = e - 2 * R
        g = f - 2 * R * n_out
        first = e < 2 * R
        paired = f < 2 * R * n_out
        dist = jnp.where(
            first, e // R,
            jnp.where(paired, jnp.where(f % 2 == 0, -(f // (2 * R) + 1), f // (2 * R) + 2), n_out + 2 + g // R),
        )
        j = jnp.where(first, e % R, jnp.where(paired, (f % (2 * R)) // 2, g % R))
        return z + way * dist, flip(r, j, R), dist, j

    def block_copy(zs, rs, width, z_to, c_to, send_sem, recv_sem):
        ref = a_all.at[zs, rs, co, :, pl.ds(0, width)]
        return pltpu.make_async_remote_copy(
            src_ref=ref, dst_ref=ref, send_sem=send_sem, recv_sem=recv_sem.at[zs, rs],
            device_id=(r, z_to * 2 + c_to), device_id_type=MESH,
        )

    def by_width(head_only, fn):
        if F == 0:
            fn(Kr)
            return

        @pl.when(head_only)
        def _():
            fn(H)

        @pl.when(jnp.logical_not(head_only))
        def _():
            fn(Kr)

    def forward(e, act):
        zs, rs, _, _ = event(e)

        def right(width):
            act(block_copy(zs, rs, width, z + 1, co, right_send.at[zs, rs], own_recv))

        def left(width):
            act(block_copy(zs, rs, width, z - 1, co, left_send.at[zs, rs], own_recv))

        def mate(width):
            act(block_copy(zs, rs, width, z, 1 - co, mate_send.at[zs, rs], mate_recv))

        @pl.when((zs <= z) & (z < Z - 1))
        def _():
            by_width(z + 1 == Z - 1, right)

        @pl.when((zs >= z) & (z > 0))
        def _():
            by_width(z - 1 == 0, left)

        by_width(at_end & (zs != z), mate)

    def await_block(e, sem, core):
        zs, rs, _, _ = event(e)

        def wait(width):
            ref = a_all.at[zs, rs, core, :, pl.ds(0, width)]
            pltpu.make_async_copy(ref, ref, sem.at[zs, rs]).wait()

        by_width(at_end & (zs != z), wait)

    def product(zs, rs, start, width, hi, lo):
        x = a_all[zs, rs, :, :, start:start + width].reshape(rows, width)
        x_hi, x_lo = split2(x)
        return dot(x_hi, hi) + (dot(x_lo, hi) + dot(x_hi, lo))

    def slot_copy(zs, rs):
        return pltpu.make_async_remote_copy(
            src_ref=part.at[zs, rs], dst_ref=slots.at[zs, r], send_sem=slot_send.at[zs, rs],
            recv_sem=slot_recv.at[zs, r], device_id=(rs, c), device_id_type=MESH,
        )

    def off_copy(zs, rs):
        return pltpu.make_async_remote_copy(
            src_ref=off_part.at[zs, rs], dst_ref=off_slots.at[zs, r], send_sem=off_send.at[zs, rs],
            recv_sem=off_recv.at[zs, r], device_id=(rs, c), device_id_type=MESH,
        )

    def sum_copy(zs):
        return pltpu.make_async_remote_copy(
            src_ref=off_sum.at[zs], dst_ref=slots.at[zs, R], send_sem=sum_send.at[zs],
            recv_sem=slot_recv.at[zs, R], device_id=(r, end_z * 2 + co), device_id_type=MESH,
        )

    def off_product(zs, rs):
        off_part[zs, rs] = product(zs, rs, H, F, off_hi[...], off_lo[...])

        @pl.when(rs != r)
        def _():
            off_copy(zs, rs).start()

    def compute(e):
        zs, rs, dist, j = event(e)
        await_block(e, mate_recv, 1 - co)

        def main(width):
            part[zs, rs] = product(zs, rs, 0, width, b_hi[0:width, :], b_lo[0:width, :])

        by_width(at_end & (zs != z), main)

        @pl.when(rs != r)
        def _():
            slot_copy(zs, rs).start()

        if F:
            @pl.when(beside_end & (dist == -1))
            def _():
                @pl.when(j == 0)
                def _():
                    pltpu.make_async_copy(off_raw, off_raw, b_recv).wait()
                    off_hi[...], off_lo[...] = split2(off_raw[...])

                off_product(z, rs)
                off_product(z + way, rs)

            @pl.when(beside_end & (dist >= 2))
            def _():
                off_product(zs, rs)

    def reduce_off(zs):
        total = off_part[zs, r]
        for k in range(1, R):
            other = flip(r, k, R)
            ref = off_slots.at[zs, other]
            pltpu.make_async_copy(ref, ref, off_recv.at[zs, other]).wait()
            total = total + off_slots[zs, other]
        off_sum[zs] = total
        sum_copy(zs).start()

    def b_tail_copy():
        return pltpu.make_async_remote_copy(
            src_ref=integrals.at[pl.ds(H, F), :], dst_ref=off_raw, send_sem=b_send, recv_sem=b_recv,
            device_id=(r, (end_z + way) * 2 + co), device_id_type=MESH,
        )

    def swap_copy(k):
        other = flip(r, k, R)
        return pltpu.make_async_remote_copy(
            src_ref=amps.at[:, pl.ds(pl.multiple_of(other * Kr, 128), Kr)], dst_ref=a_all.at[z, r, co],
            send_sem=swap_send.at[k], recv_sem=own_recv.at[z, r], device_id=(other, c), device_id_type=MESH,
        )

    mine = pltpu.make_async_copy(
        amps.at[:, pl.ds(pl.multiple_of(r * Kr, 128), Kr)], a_all.at[z, r, co], own_recv.at[z, r]
    )
    mine.start()
    load_b = pltpu.make_async_copy(integrals, b_raw, load_sem)
    load_b.start()

    barrier = pltpu.get_barrier_semaphore()

    def greet(device):
        pl.semaphore_signal(barrier, inc=1, device_id=device, device_id_type=MESH)

    for k in range(1, R):
        greet((flip(r, k, R), c))
    greet((r, z * 2 + 1 - co))

    @pl.when(z > 0)
    def _():
        greet((r, c - 2))

    @pl.when(z < Z - 1)
    def _():
        greet((r, c + 2))

    pl.semaphore_wait(barrier, R + (z > 0).astype(jnp.int32) + (z < Z - 1).astype(jnp.int32))

    for k in range(1, R):
        swap_copy(k).start()
    if F:
        @pl.when(at_end)
        def _():
            b_tail_copy().start()

    def start(copy):
        copy.start()

    await_block(0, own_recv, co)
    forward(0, start)
    load_b.wait()
    b_hi[...], b_lo[...] = split2(b_raw[...])

    @pl.loop(1, E)
    def _(e):
        await_block(e, own_recv, co)
        forward(e, start)
        compute(e - 1)

    if F:
        @pl.when(beside_end)
        def _():
            reduce_off(z)
            reduce_off(z + way)

    compute(E - 1)
    if F:
        @pl.when(beside_end)
        def _():
            for d in range(2, Z - 1):
                reduce_off(z + way * d)

    for zs in range(Z):
        total = part[zs, r]
        for k in range(1, R):
            other = flip(r, k, R)
            ref = slots.at[zs, other]
            pltpu.make_async_copy(ref, ref, slot_recv.at[zs, other]).wait()
            total = total + slots[zs, other]
        ladder[zs * rows:(zs + 1) * rows, :] = total
        if F:
            @pl.when(at_end & (z != zs))
            def _(zs=zs):
                ref = slots.at[zs, R]
                pltpu.make_async_copy(ref, ref, slot_recv.at[zs, R]).wait()
                ladder[zs * rows:(zs + 1) * rows, :] += slots[zs, R]

    G = out.shape[0]
    place = (lax.broadcasted_iota(jnp.int32, (G, G), 0) == owner[pl.ds(r, 1), :]).astype(jnp.float32).astype(jnp.bfloat16)
    x = ladder[...]
    h0 = x.astype(jnp.bfloat16)
    x = x - h0.astype(jnp.float32)
    h1, h2 = split2(x)
    placed = (dot(place, h2) + dot(place, h1)) + dot(place, h0)
    diagonal = lax.broadcasted_iota(jnp.int32, (G, G), 0) == lax.broadcasted_iota(jnp.int32, (G, G), 1)
    occ_column = jnp.sum(jnp.where(diagonal, occ[...], 0.0), axis=1, keepdims=True)
    out[...] = placed / (vir[...] - occ_column)

    def wait_send(copy):
        copy.wait_send()

    for k in range(1, R):
        swap_copy(k).wait_send()
    if F:
        @pl.when(at_end)
        def _():
            b_tail_copy().wait_send()

    @pl.loop(0, E)
    def _(e):
        zs, rs, dist, j = event(e)
        forward(e, wait_send)

        @pl.when(rs != r)
        def _():
            slot_copy(zs, rs).wait_send()

        if F:
            @pl.when(beside_end & (dist != -1))
            def _():
                @pl.when(rs != r)
                def _():
                    off_copy(zs, rs).wait_send()

                @pl.when(j == 0)
                def _():
                    sum_copy(zs).wait_send()


def solution(mesh):
    R, C = mesh.shape["row"], mesh.shape["col"]
    Z = C // 2

    def per_device(amps, row_owner, integrals, occ, vir):
        D = amps.shape[0]
        Kr, N = integrals.shape
        F = Kr * TAIL_PART[0] // TAIL_PART[1] // 128 * 128 if Z >= 4 else 0
        f = max(F, 128)
        G = occ.shape[0]
        rows = 2 * D
        f32, bf16 = jnp.float32, jnp.bfloat16
        dma = pltpu.SemaphoreType.DMA
        vmem = pl.BlockSpec(memory_space=pltpu.VMEM)
        hbm = pl.BlockSpec(memory_space=pl.ANY)
        return pl.pallas_call(
            functools.partial(kernel, R, Z, F),
            out_shape=jax.ShapeDtypeStruct((G, N), f32),
            in_specs=[hbm, vmem, hbm, vmem, vmem],
            out_specs=vmem,
            scratch_shapes=[
                pltpu.VMEM((Z, R, 2, D, Kr), f32),
                pltpu.VMEM((Kr, N), f32),
                pltpu.VMEM((Kr, N), bf16),
                pltpu.VMEM((Kr, N), bf16),
                pltpu.VMEM((Z, R, rows, N), f32),
                pltpu.VMEM((Z, R + 1, rows, N), f32),
                pltpu.VMEM((G, N), f32),
                pltpu.VMEM((f, N), f32),
                pltpu.VMEM((f, N), bf16),
                pltpu.VMEM((f, N), bf16),
                pltpu.VMEM((Z, R, rows, N), f32),
                pltpu.VMEM((Z, R, rows, N), f32),
                pltpu.VMEM((Z, rows, N), f32),
                dma((Z, R)), dma((Z, R)), dma((Z, R + 1)),
                dma((Z, R)), dma((Z, R)), dma((Z, R)), dma((Z, R)), dma((R,)), dma,
                dma((Z, R)), dma((Z, R)), dma((Z,)), dma, dma,
            ],
            compiler_params=pltpu.CompilerParams(
                collective_id=0, has_side_effects=True, vmem_limit_bytes=48 * 1024 * 1024
            ),
        )(amps, row_owner, integrals, occ.reshape(1, -1), vir.reshape(1, -1))

    return jax.shard_map(
        per_device,
        mesh=mesh,
        in_specs=(P(("row", "col"), None), P(), P("row", "col"), P("row"), P("col")),
        out_specs=P("row", "col"),
        check_vma=False,
    )
```

time: 166 us -> 71 us (0.43)
  waiting for transfers between devices: 130 us -> 0 us
  Pallas kernels: 0 us -> 65.4 us
  between operations: 13.4 us -> 0.01 us
  matrix products: 10.6 us -> 0 us
  starting transfers between devices: 6.36 us -> 0 us
    all_gather x2 -> x0, waiting for transfers between devices: 109 us -> none  [the longest x1 66.4 us: per_device(): amplitudes = lax.all_gather(ordered, 'col', axis=1, tiled=True)]
    pallas_call x0 -> x1, Pallas kernels: none -> 65.4 us  [per_device(): pl.pallas_call(functools.partial(kernel, R, Z, F), out_shape=jax.ShapeDty...]
    all_to_all x1 -> x0, waiting for transfers between devices: 20.2 us -> none  [per_device(): lax.all_to_all(source_amps, 'col', split_axis=1, concat_axis=0, tiled=True)]
    dot_general x1 -> x0, matrix products: 10.6 us -> none  [per_device(): jnp.dot(amplitudes, lax.all_gather(integrals, 'row', axis=0, tiled=True),...]
    all_to_all x1 -> x0, starting transfers between devices: 6.33 us -> none  [per_device(): lax.all_to_all(source_amps, 'col', split_axis=1, concat_axis=0, tiled=True)]
    unnamed x4 -> x11, local copies, waits for them, and re-layouts: 0.01 us -> 5.29 us
    scatter x1 -> x0, local copies, waits for them, and re-layouts: 2.36 us -> none  [place_rows(): return jnp.zeros_like(block_rows).at[owners].set(block_rows)]
    all_to_all x1 -> x0, local copies, waits for them, and re-layouts: 2.1 us -> none  [per_device(): lax.all_to_all(source_amps, 'col', split_axis=1, concat_axis=0, tiled=True)]
  transfers between devices with their start and end apart: 3 -> 0, of which waited for: 3 -> 0; matrix products, arithmetic and copies ran while one was open for 3% -> 0% of each run, Pallas kernels for 0% -> 0%
where the time goes in v1:
time: 71 us; the launch traced here: 70.7 us
  Pallas kernels  65.4 us (92%)
  local copies, waits for them, and re-layouts  5.29 us (7%)
    pallas_call x1, Pallas kernels, per_device(): pl.pallas_call(functools.partial(kernel, R, Z, F), out_shape=jax.ShapeDty...  65.4 us
    unnamed x11, local copies, waits for them, and re-layouts  5.29 us

profile of v1, /device:TPU:0, one launch (start us, length us, event | category | flops | bytes accessed | tf_op | source)
XLA Modules:
  0.0 70.7 jit_solution(13233175964775102829)
XLA Ops:
  0.0 0.0 copy-start
  0.0 1.4 %copy-done = f32[1536,256]{1,0:T(8,128)S(1)} copy-done((f32[1536,256]{1,0:T(8,128)S(1)}, f32[1536,256]{1,0:T(8,128)}, u32[]{:S(2)}) %copy-start) | copy-done | bytes 1572888
  1.4 0.0 copy-start.1
  1.4 1.1 %copy-done.1 = f32[32,6144]{1,0:T(8,128)S(1)} copy-done((f32[32,6144]{1,0:T(8,128)S(1)}, f32[32,6144]{1,0:T(8,128)}, u32[]{:S(2)}) %copy-start.1) | copy-done | bytes 786456
  2.5 0.0 copy-start.2
  2.5 0.7 copy-done.2
  3.2 0.0 copy-start.3
  3.2 0.7 copy-done.3
  3.9 0.0 copy-start.4
  3.9 0.7 copy-done.4
  4.6 65.4 %shard_map.55 = f32[256,256]{1,0:T(8,128)S(1)} custom-call(f32[32,6144]{1,0:T(8,128)S(1)} %copy-done.1, s32[4,256]{1,0:T(4,128)S(1)} %copy-done.2, f32[1536,256]{1,0:T(8,128)S(1)} %copy-done, f32[1,256]{1,0:T(1,128)S(1)} %bitcast.2, f32[1,256]{1,0:T(1,128)S(1)} %bitcast.3), custom_call_target="tpu_custom_call" | custom-call | tf_op jit(solution)/shard_map/pallas_call | solution.py:330
  70.0 0.7 copy.7
Async XLA Ops:
  0.0 1.4 %copy-start = (f32[1536,256]{1,0:T(8,128)S(1)}, f32[1536,256]{1,0:T(8,128)}, u32[]{:S(2)}) copy-start(f32[1536,256]{1,0:T(8,128)} %integrals.1) | copy-start | bytes 4718596
  1.4 1.1 %copy-start.1 = (f32[32,6144]{1,0:T(8,128)S(1)}, f32[32,6144]{1,0:T(8,128)}, u32[]{:S(2)}) copy-start(f32[32,6144]{1,0:T(8,128)} %amps.1) | copy-start | bytes 2359300
  2.5 0.7 copy-start.2
  3.2 0.7 copy-start.3
  3.9 0.7 copy-start.4

commit v2 on v1

--- a/solution.py
+++ b/solution.py
@@ -8,7 +8,7 @@
 from jax.sharding import PartitionSpec as P
 
 MESH = pl.DeviceIdType.MESH
-TAIL_PART = (0, 12)
+TAIL_PART = (5, 12)
 
 
 def split2(x):

time: 71 us -> 71 us (level)
  no operation moved by 1% of the time
where the time goes in v2:
time: 71 us; the launch traced here: 70.8 us
  Pallas kernels  65.5 us (92%)
  local copies, waits for them, and re-layouts  5.29 us (7%)
    pallas_call x1, Pallas kernels, per_device(): pl.pallas_call(functools.partial(kernel, R, Z, F), out_shape=jax.ShapeDty...  65.5 us
    unnamed x11, local copies, waits for them, and re-layouts  5.29 us

profile of v2, /device:TPU:0, one launch (start us, length us, event | category | flops | bytes accessed | tf_op | source)
XLA Modules:
  0.0 70.8 jit_solution(13457619208037550617)
XLA Ops:
  0.0 0.0 copy-start
  0.0 1.4 %copy-done = f32[1536,256]{1,0:T(8,128)S(1)} copy-done((f32[1536,256]{1,0:T(8,128)S(1)}, f32[1536,256]{1,0:T(8,128)}, u32[]{:S(2)}) %copy-start) | copy-done | bytes 1572888
  1.4 0.0 copy-start.1
  1.4 1.1 %copy-done.1 = f32[32,6144]{1,0:T(8,128)S(1)} copy-done((f32[32,6144]{1,0:T(8,128)S(1)}, f32[32,6144]{1,0:T(8,128)}, u32[]{:S(2)}) %copy-start.1) | copy-done | bytes 786456
  2.5 0.0 copy-start.2
  2.5 0.7 copy-done.2
  3.2 0.0 copy-start.3
  3.2 0.7 copy-done.3
  3.9 0.0 copy-start.4
  3.9 0.7 copy-done.4
  4.6 65.5 %shard_map.55 = f32[256,256]{1,0:T(8,128)S(1)} custom-call(f32[32,6144]{1,0:T(8,128)S(1)} %copy-done.1, s32[4,256]{1,0:T(4,128)S(1)} %copy-done.2, f32[1536,256]{1,0:T(8,128)S(1)} %copy-done, f32[1,256]{1,0:T(1,128)S(1)} %bitcast.2, f32[1,256]{1,0:T(1,128)S(1)} %bitcast.3), custom_call_target="tpu_custom_call" | custom-call | tf_op jit(solution)/shard_map/pallas_call | solution.py:330
  70.1 0.7 copy.7
Async XLA Ops:
  0.0 1.4 %copy-start = (f32[1536,256]{1,0:T(8,128)S(1)}, f32[1536,256]{1,0:T(8,128)}, u32[]{:S(2)}) copy-start(f32[1536,256]{1,0:T(8,128)} %integrals.1) | copy-start | bytes 4718596
  1.4 1.1 %copy-start.1 = (f32[32,6144]{1,0:T(8,128)S(1)}, f32[32,6144]{1,0:T(8,128)}, u32[]{:S(2)}) copy-start(f32[32,6144]{1,0:T(8,128)} %amps.1) | copy-start | bytes 2359300
  2.5 0.7 copy-start.2
  3.2 0.7 copy-start.3
  3.9 0.7 copy-start.4

commit v3 on v1

--- a/solution.py
+++ b/solution.py
@@ -31,10 +31,11 @@
 
 def kernel(
     R, Z, F,
-    amps, owner, integrals, occ, vir, out,
+    amps, owner_in, integrals, occ_in, vir_in, out,
     a_all, b_raw, b_hi, b_lo, part, slots, ladder, off_raw, off_hi, off_lo, off_part, off_slots, off_sum,
     own_recv, mate_recv, slot_recv, right_send, left_send, mate_send, slot_send, swap_send, load_sem,
     off_recv, off_send, sum_send, b_send, b_recv,
+    owner, occ, vir, small_sem,
 ):
     r = lax.axis_index("row")
     c = lax.axis_index("col")
@@ -83,7 +84,7 @@
         def _():
             fn(Kr)
 
-    def forward(e, act):
+    def forward(e, act, parts):
         zs, rs, _, _ = event(e)
 
         def right(width):
@@ -95,15 +96,25 @@
         def mate(width):
             act(block_copy(zs, rs, width, z, 1 - co, mate_send.at[zs, rs], mate_recv))
 
-        @pl.when((zs <= z) & (z < Z - 1))
-        def _():
-            by_width(z + 1 == Z - 1, right)
-
-        @pl.when((zs >= z) & (z > 0))
-        def _():
-            by_width(z - 1 == 0, left)
-
-        by_width(at_end & (zs != z), mate)
+        def along(late):
+            held = at_end & (zs == z) if F else False
+
+            def when(cond):
+                return pl.when(cond & held if late else cond & jnp.logical_not(held))
+
+            @when((zs <= z) & (z < Z - 1))
+            def _():
+                by_width(z + 1 == Z - 1, right)
+
+            @when((zs >= z) & (z > 0))
+            def _():
+                by_width(z - 1 == 0, left)
+
+        if parts != "late":
+            along(False)
+            by_width(at_end & (zs != z), mate)
+        if parts != "now" and F:
+            along(True)
 
     def await_block(e, sem, core):
         zs, rs, _, _ = event(e)
@@ -201,6 +212,12 @@
     mine.start()
     load_b = pltpu.make_async_copy(integrals, b_raw, load_sem)
     load_b.start()
+    small = [
+        pltpu.make_async_copy(src, dst, small_sem.at[i])
+        for i, (src, dst) in enumerate(((owner_in, owner), (occ_in, occ), (vir_in, vir)))
+    ]
+    for copy in small:
+        copy.start()
 
     barrier = pltpu.get_barrier_semaphore()
 
@@ -232,14 +249,28 @@
         copy.start()
 
     await_block(0, own_recv, co)
-    forward(0, start)
+    forward(0, start, "now")
     load_b.wait()
+    for copy in small:
+        copy.wait()
     b_hi[...], b_lo[...] = split2(b_raw[...])
 
     @pl.loop(1, E)
     def _(e):
+        if F:
+            late = e - 2 * R
+            slot = (2 * late + 2) // 3
+
+            @pl.when(at_end & (late == 0))
+            def _():
+                b_tail_copy().wait_send()
+
+            @pl.when(at_end & (late >= 0) & (slot < R) & ((3 * slot) // 2 == late))
+            def _():
+                forward(slot, start, "late")
+
         await_block(e, own_recv, co)
-        forward(e, start)
+        forward(e, start, "now")
         compute(e - 1)
 
     if F:
@@ -254,6 +285,31 @@
         def _():
             for d in range(2, Z - 1):
                 reduce_off(z + way * d)
+
+    def wait_send(copy):
+        copy.wait_send()
+
+    for k in range(1, R):
+        swap_copy(k).wait_send()
+    @pl.loop(0, E)
+    def _(e):
+        zs, rs, dist, j = event(e)
+        forward(e, wait_send, "all")
+
+        @pl.when(rs != r)
+        def _():
+            slot_copy(zs, rs).wait_send()
+
+        if F:
+            @pl.when(beside_end & (dist != -1))
+            def _():
+                @pl.when(rs != r)
+                def _():
+                    off_copy(zs, rs).wait_send()
+
+                @pl.when(j == 0)
+                def _():
+                    sum_copy(zs).wait_send()
 
     for zs in range(Z):
         total = part[zs, r]
@@ -281,36 +337,6 @@
     occ_column = jnp.sum(jnp.where(diagonal, occ[...], 0.0), axis=1, keepdims=True)
     out[...] = placed / (vir[...] - occ_column)
 
-    def wait_send(copy):
-        copy.wait_send()
-
-    for k in range(1, R):
-        swap_copy(k).wait_send()
-    if F:
-        @pl.when(at_end)
-        def _():
-            b_tail_copy().wait_send()
-
-    @pl.loop(0, E)
-    def _(e):
-        zs, rs, dist, j = event(e)
-        forward(e, wait_send)
-
-        @pl.when(rs != r)
-        def _():
-            slot_copy(zs, rs).wait_send()
-
-        if F:
-            @pl.when(beside_end & (dist != -1))
-            def _():
-                @pl.when(rs != r)
-                def _():
-                    off_copy(zs, rs).wait_send()
-
-                @pl.when(j == 0)
-                def _():
-                    sum_copy(zs).wait_send()
-
 
 def solution(mesh):
     R, C = mesh.shape["row"], mesh.shape["col"]
@@ -330,7 +356,7 @@
         return pl.pallas_call(
             functools.partial(kernel, R, Z, F),
             out_shape=jax.ShapeDtypeStruct((G, N), f32),
-            in_specs=[hbm, vmem, hbm, vmem, vmem],
+            in_specs=[hbm] * 5,
             out_specs=vmem,
             scratch_shapes=[
                 pltpu.VMEM((Z, R, 2, D, Kr), f32),
@@ -349,9 +375,10 @@
                 dma((Z, R)), dma((Z, R)), dma((Z, R + 1)),
                 dma((Z, R)), dma((Z, R)), dma((Z, R)), dma((Z, R)), dma((R,)), dma,
                 dma((Z, R)), dma((Z, R)), dma((Z,)), dma, dma,
+                pltpu.VMEM(row_owner.shape, jnp.int32), pltpu.VMEM((1, G), f32), pltpu.VMEM((1, N), f32), dma((3,)),
             ],
             compiler_params=pltpu.CompilerParams(
-                collective_id=0, has_side_effects=True, vmem_limit_bytes=48 * 1024 * 1024
+                collective_id=0, has_side_effects=True, vmem_limit_bytes=60 * 1024 * 1024
             ),
         )(amps, row_owner, integrals, occ.reshape(1, -1), vir.reshape(1, -1))
 

time: 71 us -> 67.1 us (0.945)
  local copies, waits for them, and re-layouts: 5.29 us -> 1.67 us
    unnamed x11 -> x1, local copies, waits for them, and re-layouts: 5.29 us -> 1.67 us
where the time goes in v3:
time: 67.1 us; the launch traced here: 67 us
  Pallas kernels  65.3 us (97%)
  local copies, waits for them, and re-layouts  1.67 us (2%)
    pallas_call x1, Pallas kernels, per_device(): pl.pallas_call(functools.partial(kernel, R, Z, F), out_shape=jax.ShapeDty...  65.3 us
    unnamed x1, local copies, waits for them, and re-layouts  1.67 us

profile of v3, /device:TPU:0, one launch (start us, length us, event | category | flops | bytes accessed | tf_op | source)
XLA Modules:
  0.0 67.0 jit_solution(12207724986361766291)
XLA Ops:
  0.0 65.3 %shard_map.55 = f32[256,256]{1,0:T(8,128)} custom-call(f32[32,6144]{1,0:T(8,128)} %amps.1, s32[4,256]{1,0:T(4,128)} %owner_in.1, f32[1536,256]{1,0:T(8,128)} %integrals.1, f32[1,256]{1,0:T(1,128)} %bitcast.2, f32[1,256]{1,0:T(1,128)} %bitcast.3), custom_call_target="tpu_custom_call" | custom-call | tf_op jit(solution)/shard_map/pallas_call | solution.py:356
  65.3 1.7 %copy.7 = f32[256,256]{1,0:T(8,128)} copy(f32[256,256]{1,0:T(8,128)} %shard_map.55) | data formatting | bytes 524288

commit v4 on v3

--- a/solution.py
+++ b/solution.py
@@ -62,7 +62,8 @@
             jnp.where(paired, jnp.where(f % 2 == 0, -(f // (2 * R) + 1), f // (2 * R) + 2), n_out + 2 + g // R),
         )
         j = jnp.where(first, e % R, jnp.where(paired, (f % (2 * R)) // 2, g % R))
-        return z + way * dist, flip(r, j, R), dist, j
+        turned = jnp.where(first, j, (j + 1) % R)
+        return z + way * dist, flip(r, turned, R), dist, j
 
     def block_copy(zs, rs, width, z_to, c_to, send_sem, recv_sem):
         ref = a_all.at[zs, rs, co, :, pl.ds(0, width)]

time: 67.1 us -> 65.7 us (0.979)
  Pallas kernels: 65.3 us -> 63.8 us
    pallas_call x1, Pallas kernels: 65.3 us -> 63.8 us  [per_device(): pl.pallas_call(functools.partial(kernel, R, Z, F), out_shape=jax.ShapeDty...]
where the time goes in v4:
time: 65.7 us; the launch traced here: 65.5 us
  Pallas kernels  63.8 us (97%)
  local copies, waits for them, and re-layouts  1.67 us (3%)
    pallas_call x1, Pallas kernels, per_device(): pl.pallas_call(functools.partial(kernel, R, Z, F), out_shape=jax.ShapeDty...  63.8 us
    unnamed x1, local copies, waits for them, and re-layouts  1.67 us

profile of v4, /device:TPU:0, one launch (start us, length us, event | category | flops | bytes accessed | tf_op | source)
XLA Modules:
  0.0 65.5 jit_solution(5823333669426402)
XLA Ops:
  0.0 63.8 %shard_map.55 = f32[256,256]{1,0:T(8,128)} custom-call(f32[32,6144]{1,0:T(8,128)} %amps.1, s32[4,256]{1,0:T(4,128)} %owner_in.1, f32[1536,256]{1,0:T(8,128)} %integrals.1, f32[1,256]{1,0:T(1,128)} %bitcast.2, f32[1,256]{1,0:T(1,128)} %bitcast.3), custom_call_target="tpu_custom_call" | custom-call | tf_op jit(solution)/shard_map/pallas_call | solution.py:357
  63.9 1.7 %copy.7 = f32[256,256]{1,0:T(8,128)} copy(f32[256,256]{1,0:T(8,128)} %shard_map.55) | data formatting | bytes 524288

commit v5 on v4

--- a/solution.py
+++ b/solution.py
@@ -270,9 +270,18 @@
             def _():
                 forward(slot, start, "late")
 
+        early = at_end & (e > E - R)
+
+        @pl.when(early)
+        def _():
+            compute(e - 1)
+
         await_block(e, own_recv, co)
         forward(e, start, "now")
-        compute(e - 1)
+
+        @pl.when(jnp.logical_not(early))
+        def _():
+            compute(e - 1)
 
     if F:
         @pl.when(beside_end)

time: 65.7 us -> 64 us (0.974)
  Pallas kernels: 63.8 us -> 62.1 us
    pallas_call x1, Pallas kernels: 63.8 us -> 62.1 us  [per_device(): pl.pallas_call(functools.partial(kernel, R, Z, F), out_shape=jax.ShapeDty...]
where the time goes in v5:
time: 64 us; the launch traced here: 63.7 us
  Pallas kernels  62.1 us (97%)
  local copies, waits for them, and re-layouts  1.67 us (3%)
    pallas_call x1, Pallas kernels, per_device(): pl.pallas_call(functools.partial(kernel, R, Z, F), out_shape=jax.ShapeDty...  62.1 us
    unnamed x1, local copies, waits for them, and re-layouts  1.67 us

profile of v5, /device:TPU:0, one launch (start us, length us, event | category | flops | bytes accessed | tf_op | source)
XLA Modules:
  0.0 63.7 jit_solution(3489455429659764541)
XLA Ops:
  0.0 62.1 %shard_map.55 = f32[256,256]{1,0:T(8,128)} custom-call(f32[32,6144]{1,0:T(8,128)} %amps.1, s32[4,256]{1,0:T(4,128)} %owner_in.1, f32[1536,256]{1,0:T(8,128)} %integrals.1, f32[1,256]{1,0:T(1,128)} %bitcast.2, f32[1,256]{1,0:T(1,128)} %bitcast.3), custom_call_target="tpu_custom_call" | custom-call | tf_op jit(solution)/shard_map/pallas_call | solution.py:366
  62.1 1.7 %copy.7 = f32[256,256]{1,0:T(8,128)} copy(f32[256,256]{1,0:T(8,128)} %shard_map.55) | data formatting | bytes 524288
